TPU v7x, 128 devices: a whole 4x4x4 slice. The times are simulated.
128 devices in a mesh: path: 32 (over y, z, x_lo), section: 4 (over x_hi, core).
Axes of the slice: x: 4 (x_hi: 2, x_lo: 2; x = x_hi * 2 + x_lo), y: 4, z: 4, core: 2. Of those that a mesh axis runs over, the one named last changes fastest.
Arguments:
- delta: bfloat16 [4, 32, 2048, 1024], P('section', 'path'), may hold values from -0.1796875 to 0.1796875
- outer_params: float32 [4, 16, 2048, 1024], P('section', None, 'path'), may hold values from -0.125 to 0.125
- momentum: float32 [4, 16, 2048, 1024], P('section', None, 'path'), may hold values from -0.06 to 0.06
- module_table: int32 [4, 32, 1], P('section'), may hold values from 0 to 15
- token_ids: int32 [32, 512], P('path'), may hold values from 0 to 15999
- embedding: bfloat16 [16000, 2048], P(None, 'path'), may hold values from -6 to 6
Outputs:
- new_params: float32 [4, 16, 2048, 1024], P('section', None, 'path')
- new_momentum: float32 [4, 16, 2048, 1024], P('section', None, 'path')
- level_outputs: bfloat16 [4, 32, 512, 2048], P('section', 'path')
Inputs may be any that keep to these rules, and one draw needn't show every extreme that they name: `module_table`: each value of 0 to 15 appears somewhere in the table.
All inputs are finite; a program needn't handle non-finite values.
Results may differ from a plain program's by a relative error of at most 0.0059.
Values may be sent and summed in bfloat16 or wider, within the bound.
A program may use at most 128 MiB of HBM per device.

v0:
```python
import jax
import jax.numpy as jnp
from jax import lax
from jax.sharding import PartitionSpec as P


def shifted(array, axis, by):
    length = lax.axis_size(axis)
    pairs = [(i, i + by) for i in range(length) if 0 <= i + by < length]
    return lax.ppermute(array, axis, pairs)


def apply_level(acts, weights):
    width = weights.shape[1]
    values = acts.astype(jnp.float32)
    scale = lax.rsqrt(jnp.mean(values * values, axis=-1, keepdims=True) + 1e-06)
    normed = (values * scale).astype(jnp.bfloat16)
    mixed = jnp.dot(normed, weights, preferred_element_type=jnp.float32)
    written = values[:, :width] + jax.nn.silu(mixed)
    return jnp.concatenate([written, values[:, width:]], axis=-1).astype(jnp.bfloat16)


def outer_update(pieces, params_part, moment_part, onehot, counts, chosen):
    sums = jnp.einsum("mp,prc->mrc", onehot, pieces, preferred_element_type=jnp.float32)
    grad = sums / counts[:, None, None]
    moment_next = 0.9 * moment_part + grad
    params_next = params_part - 0.7 * (grad + 0.9 * moment_next)
    outgoing = jnp.take(params_next.astype(jnp.bfloat16), chosen, axis=0)
    return (params_next, moment_next, outgoing)


def local(delta, outer_params, momentum, module_table, token_ids, embedding):
    section_index = lax.axis_index("section")
    levels = lax.axis_size("section")
    local_delta = delta[0, 0]
    chosen = module_table[0, :, 0]
    modules = outer_params.shape[1]
    matches = chosen[None, :] == jnp.arange(modules, dtype=jnp.int32)[:, None]
    counts = jnp.maximum(jnp.sum(matches.astype(jnp.float32), axis=1), 1.0)
    onehot = matches.astype(jnp.bfloat16)
    params_here = outer_params[0]
    moment_here = momentum[0]
    pieces = lax.all_to_all(local_delta[None], "path", split_axis=1, concat_axis=0, tiled=True)
    params_next, moment_next, outgoing = outer_update(
        pieces, params_here, moment_here, onehot, counts, chosen
    )
    weight = lax.all_to_all(outgoing, "path", split_axis=0, concat_axis=1, tiled=True)[0]
    all_tokens = lax.all_gather(token_ids, "path", axis=0, tiled=True)
    paths = all_tokens.shape[0]
    tok_rows = all_tokens.shape[1]
    looked = jnp.take(embedding, all_tokens.reshape(-1), axis=0).reshape(
        paths, tok_rows, embedding.shape[1]
    )
    tokens_in = lax.all_to_all(looked, "path", split_axis=0, concat_axis=2, tiled=True)[0]
    blocks = 1
    block_rows = tok_rows // blocks
    rounds = blocks + levels - 1
    model_width = tokens_in.shape[1]
    carried = jnp.zeros((block_rows, model_width), jnp.bfloat16)
    result = jnp.zeros((tok_rows, model_width), jnp.bfloat16)
    for turn in range(rounds):
        if turn < blocks:
            first = tokens_in
        else:
            first = jnp.zeros((block_rows, model_width), jnp.bfloat16)
        position = turn - section_index
        valid = (position >= 0) & (position < blocks)
        start = jnp.clip(position, 0, blocks - 1) * block_rows
        entering = jnp.where(section_index == 0, first, carried)
        leaving = apply_level(entering, weight)
        current = result
        result = jnp.where(valid, leaving, current)
        if turn + 1 < rounds:
            carried = shifted(leaving, "section", 1)
    return (params_next[None], moment_next[None], result[None, None])


def solution(mesh):
    return jax.shard_map(
        local,
        mesh=mesh,
        in_specs=(
            P("section", "path", None, None),
            P("section", None, "path", None),
            P("section", None, "path", None),
            P("section", None, None),
            P("path", None),
            P(None, "path"),
        ),
        out_specs=(
            P("section", None, "path", None),
            P("section", None, "path", None),
            P("section", "path", None, None),
        ),
        check_vma=False,
    )
```

profile of v0, /device:TPU:1, one launch (start us, length us, event | category | flops | bytes accessed | tf_op | source)
XLA Modules:
  0.0 477.6 jit_solution(5711758508285319008)
XLA Ops:
  0.6 8.6 %copy.76 = bf16[1,2048,1024]{2,0,1:T(2,128)(2,1)} copy(bf16[1,2048,1024]{2,1,0:T(8,128)(2,1)} %bitcast.80) | data formatting | bytes 8388608 | tf_op jit(solution)/shard_map/broadcast_in_dim;squeeze | solution.py:43
  9.3 0.5 broadcast.253
  9.8 26.0 %reduce.2 = bf16[2048,1024]{1,0:T(8,128)(2,1)} reduce(bf16[2048,1,1024]{2,1,0:T(2,128)(2,1)} %bitcast.74, bf16[]{:T(256)} %broadcast.253), dimensions={1}, to_apply=%bitcast.73.reduce_sub_computation | reduce | bytes 8388610
  35.8 7.8 %reshape.312 = bf16[32,2,32768]{2,1,0:T(2,128)(2,1)} reshape(bf16[2048,1024]{1,0:T(8,128)(2,1)} %reduce.2) | data formatting | bytes 8388608
  43.6 10.1 %all-to-all-start = ((bf16[32,2,32768]{2,1,0:T(2,128)(2,1)}), bf16[32,2,32768]{2,1,0:T(2,128)(2,1)}, u32[]{:S(2)}, u32[]{:S(2)}) async-start(bf16[32,2,32768]{2,1,0:T(2,128)(2,1)} %reshape.312), calls=%async_computation | async-start | bytes 8388608 | tf_op jit(solution)/shard_map/all_to_all | solution.py:43
  53.7 117.3 %all-gather = s32[32,1,512]{2,1,0:T(1,128)S(1)} all-gather(s32[1,1,512]{2,1,0:T(1,128)S(1)} %bitcast.88), channel_id=1, replica_groups=mesh['path'=32,'section'=4] {'path'}, dimensions={0}, use_global_device_ids=true | all-gather | bytes 67584 | tf_op jit(solution)/shard_map/all_gather | solution.py:48
  171.0 3.2 copy.39
  174.3 58.1 %gather_fusion = bf16[16384,64]{1,0:T(8,128)(2,1)} fusion(bf16[16000,64]{1,0:T(8,128)(2,1)} %copy.39, s32[16384]{0:T(1024)S(1)} %broadcast_clamp_fusion), kind=kCustom, calls=%fused_computation | custom fusion | bytes 4259840 | tf_op jit(solution)/shard_map/jit(_take)/gather | solution.py:51
  232.5 3.5 copy.40
  236.2 1.5 broadcast_select_fusion.1
  237.7 4.2 all-to-all-start.1
  241.9 19.8 %reshape.313 = bf16[2048,1,1024]{2,1,0:T(2,128)(2,1)} reshape(bf16[32,2,32768]{2,1,0:T(2,128)(2,1)} %all-to-all-done) | data formatting | bytes 8388608
  261.7 5.3 %copy.46 = bf16[1,2048,1024]{2,1,0:T(8,128)(2,1)S(1)} copy(bf16[1,2048,1024]{2,0,1:T(2,128)(2,1)} %bitcast.75) | data formatting | bytes 8388608
  267.0 0.5 copy-done.8
  267.6 10.3 %fusion.28 = (bf16[16,64,1024]{2,0,1:T(8,128)(2,1)S(1)}, f32[1,16,64,1024]{3,1,2,0:T(8,128)}, f32[1,16,64,1024]{3,1,2,0:T(8,128)}) fusion(f32[1,16,64,1024]{3,2,1,0:T(8,128)S(1)} %copy-done.7, f32[1,16,64,1024]{3,2,1,0:T(8,128)S(1)} %copy-done.8, f32[16]{0:T(128)S(1)} %broadcast_maximum_fusion, bf16[32,64,1024]{2,1,0:T(8,128)(2,1)S(1)} %bitcast.81, ...), kind=kOutput, calls=%fused_computation.75 | convolution fusion | flops 75497984 | bytes 23068864 | tf_op jit(solution)/shard_map/mp,prc->mrc/dot_general | solution.py:24
  277.9 2.5 copy.42
  280.4 4.4 gather_fusion.1
  284.8 4.7 broadcast_select_fusion
  289.5 8.2 %all-to-all-start.2 = ((bf16[32,64,1024]{2,1,0:T(8,128)(2,1)}), bf16[32,64,1024]{2,1,0:T(8,128)(2,1)}, u32[]{:S(2)}, u32[]{:S(2)}) async-start(bf16[32,64,1024]{2,1,0:T(8,128)(2,1)} %broadcast_select_fusion), calls=%async_computation.2 | async-start | bytes 8388608 | tf_op jit(solution)/shard_map/all_to_all | solution.py:47
  297.9 1.2 slice.38
  299.1 1.5 slice.37
  300.6 1.5 copy.49
  302.1 2.9 copy.48
  305.0 0.6 multiply_reduce_fusion.3
  305.7 1.9 multiply_convert_fusion.3
  307.5 43.2 %all-to-all-done.2 = bf16[32,64,1024]{2,1,0:T(8,128)(2,1)} async-done(((bf16[32,64,1024]{2,1,0:T(8,128)(2,1)}), bf16[32,64,1024]{2,1,0:T(8,128)(2,1)}, u32[]{:S(2)}, u32[]{:S(2)}) %all-to-all-start.2) | async-done | bytes 4194336 | tf_op jit(solution)/shard_map/all_to_all | solution.py:47
  350.7 6.1 %add_convert_fusion = bf16[512,1024]{1,0:T(8,128)(2,1)S(1)} fusion(f32[512,1024]{1,0:T(8,128)} %copy.48, bf16[512,2048]{0,1:T(8,128)(2,1)} %bitcast.85, bf16[2048,1024]{1,0:T(8,128)(2,1)} %bitcast.19), kind=kOutput, calls=%fused_computation.41 | convolution fusion | flops 2150629376 | bytes 9437184 | tf_op jit(solution)/shard_map/dot_general | solution.py:18
  357.0 12.6 %collective-permute-start = (bf16[512,2048]{1,0:T(8,128)(2,1)S(1)}, bf16[512,2048]{1,0:T(8,128)(2,1)S(1)}, u32[]{:S(2)}, u32[]{:S(2)}) collective-permute-start(bf16[512,2048]{1,0:T(8,128)(2,1)S(1)} %pad_maximum_fusion), channel_id=1, source_target_pairs={{0,1},{1,2},{2,3},{4,5},{5,6},{6,7},{8,9},{9,10},{10,11},{12,13},{... | collective-permute-start | bytes 6291464 | tf_op jit(solution)/shard_map/ppermute | solution.py:10
  369.6 23.0 %collective-permute-done = bf16[512,2048]{1,0:T(8,128)(2,1)S(1)} collective-permute-done((bf16[512,2048]{1,0:T(8,128)(2,1)S(1)}, bf16[512,2048]{1,0:T(8,128)(2,1)S(1)}, u32[]{:S(2)}, u32[]{:S(2)}) %collective-permute-start) | collective-permute-done | bytes 2097184 | tf_op jit(solution)/shard_map/ppermute | solution.py:10
  392.6 0.6 multiply_reduce_fusion.2
  393.2 0.3 fusion.17
  393.6 6.2 %fusion.7 = bf16[512,1024]{1,0:T(8,128)(2,1)S(1)} fusion(f32[512,2048]{1,0:T(8,128)S(1)} %fusion.17, bf16[2048,1024]{1,0:T(8,128)(2,1)} %bitcast.19, f32[512]{0:T(512)S(1)} %add_rsqrt_fusion.2, bf16[512,2048]{1,0:T(8,128)(2,1)S(1)} %collective-permute-done, pred[]{:T(512)S(6)} %eq.25), kind=kOutput, calls=%fused_computation.26 | convolution fusion | flops 2154823680 | bytes 9439233 | tf_op jit(solution)/shard_map/dot_general | solution.py:18
  400.1 5.9 %collective-permute-start.1 = (bf16[512,2048]{1,0:T(8,128)(2,1)S(1)}, bf16[512,2048]{1,0:T(8,128)(2,1)S(1)}, u32[]{:S(2)}, u32[]{:S(2)}) collective-permute-start(bf16[512,2048]{1,0:T(8,128)(2,1)S(1)} %pad_maximum_fusion.1), channel_id=1, source_target_pairs={{0,1},{1,2},{2,3},{4,5},{5,6},{6,7},{8,9},{9,10},{10,11},{12,13},{... | collective-permute-start | bytes 6291464 | tf_op jit(solution)/shard_map/ppermute | solution.py:10
  406.0 23.0 %collective-permute-done.1 = bf16[512,2048]{1,0:T(8,128)(2,1)S(1)} collective-permute-done((bf16[512,2048]{1,0:T(8,128)(2,1)S(1)}, bf16[512,2048]{1,0:T(8,128)(2,1)S(1)}, u32[]{:S(2)}, u32[]{:S(2)}) %collective-permute-start.1) | collective-permute-done | bytes 2097184 | tf_op jit(solution)/shard_map/ppermute | solution.py:10
  428.9 0.6 multiply_reduce_fusion.1
  429.6 0.3 fusion.18
  430.0 6.2 %fusion.6 = bf16[512,1024]{1,0:T(8,128)(2,1)S(1)} fusion(f32[512,2048]{1,0:T(8,128)S(1)} %fusion.18, bf16[2048,1024]{1,0:T(8,128)(2,1)} %bitcast.19, f32[512]{0:T(512)S(1)} %add_rsqrt_fusion.1, bf16[512,2048]{1,0:T(8,128)(2,1)S(1)} %collective-permute-done.1, pred[]{:T(512)S(6)} %eq.25), kind=kOutput, calls=%fused_computation.23 | convolution fusion | flops 2154823680 | bytes 9439233 | tf_op jit(solution)/shard_map/dot_general | solution.py:18
  436.3 1.7 pad_maximum_fusion.2
  438.0 6.2 %collective-permute-start.2 = (bf16[512,2048]{1,0:T(8,128)(2,1)}, bf16[512,2048]{1,0:T(8,128)(2,1)}, u32[]{:S(2)}, u32[]{:S(2)}) collective-permute-start(bf16[512,2048]{1,0:T(8,128)(2,1)} %pad_maximum_fusion.2), channel_id=1, source_target_pairs={{0,1},{1,2},{2,3},{4,5},{5,6},{6,7},{8,9},{9,10},{10,11},{12,13},{... | collective-permute-start | bytes 6291464 | tf_op jit(solution)/shard_map/ppermute | solution.py:10
  444.1 6.8 %copy.44 = f32[1,16,64,1024]{3,2,1,0:T(8,128)} copy(f32[1,16,64,1024]{3,1,2,0:T(8,128)} %get-tuple-element.18) | data formatting | bytes 8388608
  450.9 4.4 copy.45
  455.4 1.7 slice_bitcast_fusion.1
  457.1 1.7 slice_bitcast_fusion.2
  458.9 8.2 %collective-permute-done.2 = bf16[512,2048]{1,0:T(8,128)(2,1)} collective-permute-done((bf16[512,2048]{1,0:T(8,128)(2,1)}, bf16[512,2048]{1,0:T(8,128)(2,1)}, u32[]{:S(2)}, u32[]{:S(2)}) %collective-permute-start.2) | collective-permute-done | bytes 2097184 | tf_op jit(solution)/shard_map/ppermute | solution.py:10
  467.1 2.0 fusion.30
  469.1 0.5 multiply_reduce_fusion
  469.7 4.9 %fusion.19 = bf16[1,1,512,1024]{3,2,1,0:T(8,128)(2,1)S(1)} fusion(bf16[2048,1024]{1,0:T(8,128)(2,1)} %bitcast.19, f32[512]{0:T(512)S(1)} %add_rsqrt_fusion, bf16[512,2048]{1,0:T(8,128)(2,1)S(1)} %get-tuple-element.16, f32[512,2048]{1,0:T(8,128)S(1)} %get-tuple-element.15), kind=kOutput, calls=%fused_computation.51 | convolution fusion | flops 2153775104 | bytes 9439232 | tf_op jit(solution)/shard_map/dot_general | solution.py:18
  474.7 2.5 maximum_select_fusion
  (39 shorter events, 1.4 us)
Async XLA Ops:
  43.6 10.1 %copy-start.6 = (s32[1,512]{1,0:T(1,128)S(1)}, s32[1,512]{1,0:T(1,128)}, u32[]{:S(2)}) copy-start(s32[1,512]{1,0:T(1,128)} %param.10) | copy-start | bytes 6148
  43.6 127.4 %copy-start.5 = (bf16[16000,64]{0,1:T(8,128)(2,1)S(1)}, bf16[16000,64]{0,1:T(8,128)(2,1)}, u32[]{:S(2)}) copy-start(bf16[16000,64]{0,1:T(8,128)(2,1)} %param.11) | copy-start | bytes 6144004
  43.6 194.1 %all-to-all-start = ((bf16[32,2,32768]{2,1,0:T(2,128)(2,1)}), bf16[32,2,32768]{2,1,0:T(2,128)(2,1)}, u32[]{:S(2)}, u32[]{:S(2)}) async-start(bf16[32,2,32768]{2,1,0:T(2,128)(2,1)} %reshape.312), calls=%async_computation | async-start | bytes 8388608 | tf_op jit(solution)/shard_map/all_to_all | solution.py:43
  232.5 3.6 copy-start.9
  237.7 51.8 %all-to-all-start.1 = ((bf16[32,512,64]{1,2,0:T(8,128)(2,1)}), bf16[32,512,64]{1,2,0:T(8,128)(2,1)S(1)}, u32[]{:S(2)}, u32[]{:S(2)}) async-start(bf16[32,512,64]{1,2,0:T(8,128)(2,1)} %broadcast_select_fusion.1), calls=%async_computation.1 | async-start | bytes 4194304 | tf_op jit(solution)/shard_map/all_to_all | solution.py:54
  261.7 5.3 %copy-start.7 = (f32[1,16,64,1024]{3,2,1,0:T(8,128)S(1)}, f32[1,16,64,1024]{3,2,1,0:T(8,128)}, u32[]{:S(2)}) copy-start(f32[1,16,64,1024]{3,2,1,0:T(8,128)} %param.8) | copy-start | bytes 12582916
  261.7 5.9 %copy-start.8 = (f32[1,16,64,1024]{3,2,1,0:T(8,128)S(1)}, f32[1,16,64,1024]{3,2,1,0:T(8,128)}, u32[]{:S(2)}) copy-start(f32[1,16,64,1024]{3,2,1,0:T(8,128)} %param.7) | copy-start | bytes 12582916
  289.5 61.3 %all-to-all-start.2 = ((bf16[32,64,1024]{2,1,0:T(8,128)(2,1)}), bf16[32,64,1024]{2,1,0:T(8,128)(2,1)}, u32[]{:S(2)}, u32[]{:S(2)}) async-start(bf16[32,64,1024]{2,1,0:T(8,128)(2,1)} %broadcast_select_fusion), calls=%async_computation.2 | async-start | bytes 8388608 | tf_op jit(solution)/shard_map/all_to_all | solution.py:47
  357.0 35.5 %collective-permute-start = (bf16[512,2048]{1,0:T(8,128)(2,1)S(1)}, bf16[512,2048]{1,0:T(8,128)(2,1)S(1)}, u32[]{:S(2)}, u32[]{:S(2)}) collective-permute-start(bf16[512,2048]{1,0:T(8,128)(2,1)S(1)} %pad_maximum_fusion), channel_id=1, source_target_pairs={{0,1},{1,2},{2,3},{4,5},{5,6},{6,7},{8,9},{9,10},{10,11},{12,13},{... | collective-permute-start | bytes 6291464 | tf_op jit(solution)/shard_map/ppermute | solution.py:10
  393.5 6.4 %copy-start = (f32[512,2048]{1,0:T(8,128)}, f32[512,2048]{1,0:T(8,128)S(1)}, u32[]{:S(2)}) copy-start(f32[512,2048]{1,0:T(8,128)S(1)} %fusion.17) | copy-start | bytes 12582916
  400.1 28.9 %collective-permute-start.1 = (bf16[512,2048]{1,0:T(8,128)(2,1)S(1)}, bf16[512,2048]{1,0:T(8,128)(2,1)S(1)}, u32[]{:S(2)}, u32[]{:S(2)}) collective-permute-start(bf16[512,2048]{1,0:T(8,128)(2,1)S(1)} %pad_maximum_fusion.1), channel_id=1, source_target_pairs={{0,1},{1,2},{2,3},{4,5},{5,6},{6,7},{8,9},{9,10},{10,11},{12,13},{... | collective-permute-start | bytes 6291464 | tf_op jit(solution)/shard_map/ppermute | solution.py:10
  429.9 6.4 %copy-start.1 = (f32[512,2048]{1,0:T(8,128)}, f32[512,2048]{1,0:T(8,128)S(1)}, u32[]{:S(2)}) copy-start(f32[512,2048]{1,0:T(8,128)S(1)} %fusion.18) | copy-start | bytes 12582916
  436.3 1.7 copy-start.3
  438.0 29.2 %collective-permute-start.2 = (bf16[512,2048]{1,0:T(8,128)(2,1)}, bf16[512,2048]{1,0:T(8,128)(2,1)}, u32[]{:S(2)}, u32[]{:S(2)}) collective-permute-start(bf16[512,2048]{1,0:T(8,128)(2,1)} %pad_maximum_fusion.2), channel_id=1, source_target_pairs={{0,1},{1,2},{2,3},{4,5},{5,6},{6,7},{8,9},{9,10},{10,11},{12,13},{... | collective-permute-start | bytes 6291464 | tf_op jit(solution)/shard_map/ppermute | solution.py:10
  444.1 6.8 %copy-start.2 = (f32[1,16,64,1024]{3,1,2,0:T(8,128)S(1)}, f32[1,16,64,1024]{3,1,2,0:T(8,128)}, u32[]{:S(2)}) copy-start(f32[1,16,64,1024]{3,1,2,0:T(8,128)} %get-tuple-element.19) | copy-start | bytes 12582916
  469.7 4.9 %copy-start.4 = (bf16[512,1024]{1,0:T(8,128)(2,1)S(1)}, bf16[512,1024]{1,0:T(8,128)(2,1)}, u32[]{:S(2)}) copy-start(bf16[512,1024]{1,0:T(8,128)(2,1)} %copy-done.3) | copy-start | bytes 3145732
where the time goes:
time: 484 us; the launch traced here: 478 us
  local copies, waits for them, and re-layouts  137 us (28%)
  blocking collectives  117 us (24%)
  waiting for transfers between devices  97.4 us (20%)
  starting transfers between devices  47 us (10%)
  other arithmetic  44 us (9%)
  matrix products  33.8 us (7%)
    all_gather x1, blocking collectives, local(): all_tokens = lax.all_gather(token_ids, 'path', axis=0, tiled=True)  117 us
    gather x2, local copies, waits for them, and re-layouts, local(): jnp.take(embedding, all_tokens.reshape(-1), axis=0)  61.7 us
    ppermute x3, waiting for transfers between devices, shifted(): return lax.ppermute(array, axis, pairs)  54.2 us
    unnamed x29, local copies, waits for them, and re-layouts  52.8 us
    all_to_all x1, waiting for transfers between devices, local(): lax.all_to_all(outgoing, 'path', split_axis=0, concat_axis=1, tiled=True)[0]  43.2 us
    unnamed x1, other arithmetic  26 us
    ppermute x3, starting transfers between devices, shifted(): return lax.ppermute(array, axis, pairs)  24.6 us
    dot_general x4, matrix products, apply_level(): mixed = jnp.dot(normed, weights, preferred_element_type=jnp.float32)  23.5 us
  transfers between devices with their start and end apart: 6, of which 4 were waited for; matrix products, arithmetic and copies ran while one was open for 29% of the time, Pallas kernels for 0%

commit v1 on v0

v1 whole, which is shorter than its diff:
```python
import functools

import jax
import jax.numpy as jnp
from jax import lax
from jax.experimental import pallas as pl
from jax.experimental.pallas import tpu as pltpu
from jax.sharding import PartitionSpec as P

MESH = pl.DeviceIdType.MESH
STEPS = [(y, z, x) for y in range(4) for z in range(4) for x in range(2)][1:]
ORDER = sorted(STEPS, key=lambda t: ((t[0] * 5 + t[1] * 3 + t[2] * 7) % 11, t))


def shifted(me, step):
    y, z, x = step
    return (
        lax.rem(me // 8 + y, 4) * 8
        + lax.rem(lax.rem(me // 2, 4) + z, 4) * 2
        + lax.rem(lax.rem(me, 2) + x, 2)
    )


def kernel(
    delta, params, moment, table_t, ids, chosen,
    out_params, out_moment, out_acts,
    pieces, par, mom, fresh, sending, weight,
    columns, table, id_own, id_all, id_scalar, gathered, leaving, arrived,
    x_first, x_rest, o_first, partial,
    local_sem, id_sem, delta_send, delta_recv, weight_send, weight_recv,
    lookup_send, lookup_recv, core_sem, level_send, level_recv,
):
    me = lax.axis_index("path")
    sec = lax.axis_index("section")
    half = lax.rem(sec, 2)
    mate = sec + 1 - 2 * half
    paths, rows = pieces.shape[0], pieces.shape[1]
    modules = par.shape[0]
    wide = par.shape[2]
    width = table.shape[1]
    others = paths - 1
    late = sec >= 2

    def remote(src, dst, send, recv, path, section):
        return pltpu.make_async_remote_copy(
            src_ref=src, dst_ref=dst, send_sem=send, recv_sem=recv,
            device_id=(path, section), device_id_type=MESH,
        )

    loads = [
        pltpu.make_async_copy(table_t, columns, local_sem.at[0]),
        pltpu.make_async_copy(params, par, local_sem.at[1]),
        pltpu.make_async_copy(moment, mom, local_sem.at[2]),
    ]
    for load in loads:
        load.start()
    tiles = ids.shape[1] // 128
    for tile in range(tiles):
        id_own[tile:tile + 1, :] = ids[:, 128 * tile:128 * (tile + 1)]
    id_own[tiles:, :] = jnp.zeros((8 - tiles, 128), jnp.int32)
    id_all[me] = id_own[...]

    barrier = pltpu.get_barrier_semaphore()
    for step in ORDER:
        pl.semaphore_signal(barrier, inc=1, device_id=(shifted(me, step), sec), device_id_type=MESH)

    @pl.when(sec > 0)
    def _():
        pl.semaphore_signal(barrier, inc=1, device_id=(me, sec - 1), device_id_type=MESH)

    @pl.when(sec < 3)
    def _():
        pl.semaphore_signal(barrier, inc=1, device_id=(me, sec + 1), device_id_type=MESH)

    pl.semaphore_wait(barrier, others + jnp.where(sec > 0, 1, 0) + jnp.where(sec < 3, 1, 0))

    for step in ORDER:
        to = shifted(me, step)
        remote(id_own, id_all.at[me], id_sem.at[0], id_sem.at[1], to, sec).start()
    part = rows // 2
    for piece in range(2):
        span = pl.ds(piece * part, part)
        for step in ORDER:
            to = shifted(me, step)
            remote(
                delta.at[to, span], pieces.at[me, span],
                delta_send.at[piece], delta_recv.at[piece], to, sec,
            ).start()
        pltpu.make_async_copy(delta.at[me, span], pieces.at[me, span], local_sem.at[3 + piece]).start()

    loads[0].wait()

    @pl.loop(0, table.shape[0] // 128)
    def _(block):
        start = pl.multiple_of(block * 128, 128)
        table[pl.ds(start, 128), :] = columns[:, pl.ds(start, 128)].astype(jnp.float32).T

    everyone = id_all.at[pl.ds(0, others)]
    remote(everyone, everyone, id_sem.at[0], id_sem.at[1], me, sec).wait_recv()
    ids_in = pltpu.make_async_copy(id_all, id_scalar, local_sem.at[5])
    ids_in.start()
    ids_in.wait()

    tokens = gathered.shape[0]
    holds = jnp.logical_or(sec < 2, me >= paths // 2)
    own_rows = pl.ds(pl.multiple_of(me * width, width), width)

    @pl.when(holds)
    def _():
        @pl.loop(0, paths)
        def _(turn):
            to = shifted(me, (turn // 8, lax.rem(turn // 2, 4), lax.rem(turn, 2)))

            @pl.loop(0, tokens // 16)
            def _(group):
                line = half * (tokens // 128) + group // 8
                first = lax.rem(group, 8) * 16
                for at in range(16):
                    token = id_scalar[to, line, first + at]
                    gathered[pl.ds(group * 16 + at, 1), :] = table[pl.ds(token, 1), :]

            leaving[to] = gathered[...].T.astype(jnp.bfloat16)

            @pl.when(turn > 0)
            def _():
                remote(
                    leaving.at[to], arrived.at[half, own_rows],
                    lookup_send, lookup_recv, to, sec,
                ).start()

        arrived[half, own_rows, :] = leaving[me]

    loads[1].wait()
    loads[2].wait()
    group_rows = 16
    pair_rows, pair_cols = modules * group_rows, paths * group_rows
    col = lax.broadcasted_iota(jnp.int32, (1, pair_cols), 1)
    uses = jnp.zeros((1, pair_cols), jnp.int32)
    for path in range(paths):
        uses = jnp.where(col // group_rows == path, chosen[path], uses)
    row = lax.broadcasted_iota(jnp.int32, (pair_rows, pair_cols), 0)
    cols = lax.broadcasted_iota(jnp.int32, (pair_rows, pair_cols), 1)
    match = (uses == row // group_rows) & (lax.rem(row, group_rows) == lax.rem(cols, group_rows))
    match = match.astype(jnp.float32)
    counts = jnp.maximum(jnp.sum(match, axis=1, keepdims=True), 1.0)
    match = match.astype(jnp.bfloat16)
    lanes = 256
    for piece in range(2):
        span = pl.ds(piece * part, part)
        landed = pieces.at[pl.ds(0, others), span]
        remote(landed, landed, delta_send.at[piece], delta_recv.at[piece], me, sec).wait_recv()
        pltpu.make_async_copy(delta.at[me, span], pieces.at[me, span], local_sem.at[3 + piece]).wait()
        for group in range(part // group_rows):
            at = pl.ds(piece * part + group * group_rows, group_rows)

            @pl.loop(0, wide // lanes)
            def _(block):
                cut = pl.ds(pl.multiple_of(block * lanes, lanes), lanes)
                terms = pieces[:, at, cut].reshape(pair_cols, lanes)
                sums = jnp.dot(match, terms, preferred_element_type=jnp.float32)
                grad = sums / counts
                moved = 0.9 * mom[:, at, cut].reshape(pair_rows, lanes) + grad
                stepped = par[:, at, cut].reshape(pair_rows, lanes) - 0.7 * (grad + 0.9 * moved)
                mom[:, at, cut] = moved.reshape(modules, group_rows, lanes)
                par[:, at, cut] = stepped.reshape(modules, group_rows, lanes)
                fresh[:, at, cut] = stepped.astype(jnp.bfloat16).reshape(modules, group_rows, lanes)

        pltpu.make_async_copy(par.at[:, span], out_params.at[:, span], local_sem.at[6 + piece]).start()
        pltpu.make_async_copy(mom.at[:, span], out_moment.at[:, span], local_sem.at[8 + piece]).start()

        @pl.loop(0, paths)
        def _(path):
            sending[path, span, :] = fresh[chosen[path], span, :]

        weight[me, span, :] = sending[me, span, :]
        for step in ORDER:
            to = shifted(me, step)
            remote(
                sending.at[to, span], weight.at[me, span],
                weight_send.at[piece], weight_recv.at[piece], to, sec,
            ).start()

    def lookups(count):
        span = arrived.at[half, pl.ds(0, count * width)]
        return remote(span, span, lookup_send, lookup_recv, me, sec)

    @pl.when(sec < 2)
    def _():
        lookups(others).wait_recv()

    @pl.when(jnp.logical_and(late, me >= paths // 2))
    def _():
        lookups(paths // 2 - 1).wait_recv()

    @pl.when(jnp.logical_and(late, me < paths // 2))
    def _():
        lookups(paths // 2).wait_recv()

    model = arrived.shape[1]
    mid = model // 2
    upper = arrived.at[half, pl.ds(mid, mid)]
    lower = arrived.at[half, pl.ds(0, mid)]
    upper_copy = remote(upper, upper, core_sem.at[0], core_sem.at[1], me, mate)
    lower_copy = remote(lower, lower, core_sem.at[2], core_sem.at[3], me, mate)
    upper_copy.start()

    @pl.when(sec == 1)
    def _():
        lower_copy.start()

    other_upper = arrived.at[1 - half, pl.ds(mid, mid)]
    other_lower = arrived.at[1 - half, pl.ds(0, mid)]
    remote(other_upper, other_upper, core_sem.at[0], core_sem.at[1], me, mate).wait_recv()

    def turned(dst, first):
        for side in range(2):
            @pl.loop(0, mid // 256)
            def _(block):
                start = pl.multiple_of(block * 256, 256)
                tile = arrived[side, pl.ds(first + start, 256), :].astype(jnp.float32)
                dst[pl.ds(side * tokens, tokens), pl.ds(start, 256)] = tile.T.astype(jnp.bfloat16)

    turned(x_rest, mid)

    @pl.when(sec == 0)
    def _():
        remote(other_lower, other_lower, core_sem.at[2], core_sem.at[3], me, mate).wait_recv()
        turned(x_first, 0)

    rest_out = pltpu.make_async_copy(x_rest, out_acts.at[:, pl.ds(mid, mid)], local_sem.at[10])
    rest_out.start()

    for piece in range(2):
        span = pl.ds(piece * part, part)
        landed = weight.at[pl.ds(0, others), span]
        remote(landed, landed, weight_send.at[piece], weight_recv.at[piece], me, sec).wait_recv()

    blocks = level_send.shape[0]
    size = x_first.shape[0] // blocks
    for block in range(blocks):
        at = pl.ds(block * size, size)

        @pl.loop(0, wide // lanes)
        def _(cut_at):
            cut = pl.ds(pl.multiple_of(cut_at * lanes, lanes), lanes)
            partial[at, cut] = jnp.dot(
                x_rest[at, :], weight[paths // 2:, :, cut].reshape(mid, lanes),
                preferred_element_type=jnp.float32,
            )

    for block in range(blocks):
        at = pl.ds(block * size, size)
        here, there = x_first.at[at], o_first.at[at]
        hop = remote(there, here, level_send.at[block], level_recv.at[block], me, jnp.minimum(sec + 1, 3))

        @pl.when(sec > 0)
        def _():
            hop.wait_recv()

        firsts = x_first[at, :].astype(jnp.float32)
        rests = x_rest[at, :].astype(jnp.float32)
        squares = jnp.sum(firsts * firsts, axis=-1, keepdims=True) + jnp.sum(rests * rests, axis=-1, keepdims=True)
        scale = lax.rsqrt(squares / model + 1e-06)

        @pl.loop(0, wide // lanes)
        def _(cut_at):
            cut = pl.ds(pl.multiple_of(cut_at * lanes, lanes), lanes)
            mixed = scale * (partial[at, cut] + jnp.dot(
                x_first[at, :], weight[:paths // 2, :, cut].reshape(mid, lanes),
                preferred_element_type=jnp.float32,
            ))
            written = x_first[at, cut].astype(jnp.float32) + jax.nn.silu(mixed)
            o_first[at, cut] = written.astype(jnp.bfloat16)

        @pl.when(sec < 3)
        def _():
            hop.start()

        pltpu.make_async_copy(there, out_acts.at[at, pl.ds(0, mid)], local_sem.at[11 + block]).start()

    for block in range(blocks):
        at = pl.ds(block * size, size)
        here, there = x_first.at[at], o_first.at[at]
        hop = remote(there, here, level_send.at[block], level_recv.at[block], me, jnp.minimum(sec + 1, 3))

        @pl.when(sec < 3)
        def _():
            hop.wait_send()

        pltpu.make_async_copy(there, out_acts.at[at, pl.ds(0, mid)], local_sem.at[11 + block]).wait()
    rest_out.wait()
    remote(everyone, everyone, id_sem.at[0], id_sem.at[1], me, sec).wait_send()
    upper_copy.wait_send()

    @pl.when(sec == 1)
    def _():
        lower_copy.wait_send()

    @pl.when(holds)
    def _():
        span = leaving.at[pl.ds(0, others)]
        remote(span, span, lookup_send, lookup_recv, me, sec).wait_send()

    for piece in range(2):
        span = pl.ds(piece * part, part)
        landed = pieces.at[pl.ds(0, others), span]
        remote(landed, landed, delta_send.at[piece], delta_recv.at[piece], me, sec).wait_send()
        landed = weight.at[pl.ds(0, others), span]
        remote(landed, landed, weight_send.at[piece], weight_recv.at[piece], me, sec).wait_send()
        pltpu.make_async_copy(par.at[:, span], out_params.at[:, span], local_sem.at[6 + piece]).wait()
        pltpu.make_async_copy(mom.at[:, span], out_moment.at[:, span], local_sem.at[8 + piece]).wait()


def local(delta, outer_params, momentum, module_table, token_ids, embedding):
    paths = module_table.shape[1]
    _, modules, rows, wide = outer_params.shape
    vocab, width = embedding.shape
    tok = token_ids.shape[1]
    model = delta.shape[2]
    mid = model // 2
    blocks = 4
    bf16, f32 = jnp.bfloat16, jnp.float32
    anywhere = pl.BlockSpec(memory_space=pl.ANY)
    dma = pltpu.SemaphoreType.DMA
    new_params, new_moment, acts = pl.pallas_call(
        kernel,
        out_shape=(
            jax.ShapeDtypeStruct((modules, rows, wide), f32),
            jax.ShapeDtypeStruct((modules, rows, wide), f32),
            jax.ShapeDtypeStruct((tok, model), bf16),
        ),
        in_specs=[
            anywhere, anywhere, anywhere, anywhere,
            pl.BlockSpec(memory_space=pltpu.VMEM),
            pl.BlockSpec(memory_space=pltpu.SMEM),
        ],
        out_specs=(anywhere, anywhere, anywhere),
        scratch_shapes=[
            pltpu.VMEM((paths, rows, wide), bf16),
            pltpu.VMEM((modules, rows, wide), f32),
            pltpu.VMEM((modules, rows, wide), f32),
            pltpu.VMEM((modules, rows, wide), bf16),
            pltpu.VMEM((paths, rows, wide), bf16),
            pltpu.VMEM((paths, rows, wide), bf16),
            pltpu.VMEM((width, vocab), bf16),
            pltpu.VMEM((vocab, width), f32),
            pltpu.VMEM((8, 128), jnp.int32),
            pltpu.VMEM((paths, 8, 128), jnp.int32),
            pltpu.SMEM((paths, 8, 128), jnp.int32),
            pltpu.VMEM((tok // 2, width), f32),
            pltpu.VMEM((paths, width, tok // 2), bf16),
            pltpu.VMEM((2, model, tok // 2), bf16),
            pltpu.VMEM((tok, mid), bf16),
            pltpu.VMEM((tok, mid), bf16),
            pltpu.VMEM((tok, mid), bf16),
            pltpu.VMEM((tok, wide), f32),
            dma((16,)), dma((2,)), dma((2,)), dma((2,)), dma((2,)), dma((2,)),
            dma, dma, dma((4,)), dma((blocks,)), dma((blocks,)),
        ],
        compiler_params=pltpu.CompilerParams(
            collective_id=0, has_side_effects=True, vmem_limit_bytes=60 * 1024 * 1024,
        ),
        name="outer_step",
    )(
        delta.reshape(paths, rows, wide), outer_params[0], momentum[0],
        embedding.T, token_ids, module_table[0, :, 0],
    )
    return (new_params[None], new_moment[None], acts[None, None])


def solution(mesh):
    return jax.shard_map(
        local,
        mesh=mesh,
        in_specs=(
            P("section", "path", None, None),
            P("section", None, "path", None),
            P("section", None, "path", None),
            P("section", None, None),
            P("path", None),
            P(None, "path"),
        ),
        out_specs=(
            P("section", None, "path", None),
            P("section", None, "path", None),
            P("section", "path", None, None),
        ),
        check_vma=False,
    )
```

time: 484 us -> 154 us (0.32)
  the two profiles are of different devices: /device:TPU:1 before, /device:TPU:21 now
where the time goes in v1:
time: 154 us; the launch traced here: 152 us
  Pallas kernels  142 us (92%)
  local copies, waits for them, and re-layouts  9.37 us (6%)
    pallas_call x1, Pallas kernels, local(): pl.pallas_call(kernel, out_shape=(jax.ShapeDtypeStruct((modules, rows, wi...  142 us
    unnamed x7, local copies, waits for them, and re-layouts  9.37 us

profile of v1, /device:TPU:21, one launch (start us, length us, event | category | flops | bytes accessed | tf_op | source)
XLA Modules:
  0.0 152.1 jit_solution(7276475208673908650)
XLA Ops:
  0.6 142.1 %outer_step.1 = (f32[16,64,1024]{2,1,0:T(8,128)}, f32[16,64,1024]{2,1,0:T(8,128)}, bf16[512,2048]{1,0:T(8,128)(2,1)}) custom-call(bf16[32,64,1024]{2,1,0:T(8,128)(2,1)} %bitcast.10, f32[16,64,1024]{2,1,0:T(8,128)} %bitcast.11, f32[16,64,1024]{2,1,0:T(8,128)} %bitcast.12, bf16[64,16000]{1,0:T(8,128)(2,1)} %bitcast.14, s32[1,512]{1,0:T(1,128)} %ids.1, s32[32]{0:T(128)} %bitcast.15), custom_call_target="tpu_custom_call" | custom-call | tf_op jit(solution)/shard_map/outer_step/pallas_call | solution.py:325
  142.7 0.0 copy-start
  142.7 4.9 %copy.12 = f32[1,16,64,1024]{3,2,1,0:T(8,128)} copy(f32[1,16,64,1024]{3,2,1,0:T(8,128)} %bitcast.9) | data formatting | bytes 8388608
  147.7 0.0 copy-done
  147.7 0.0 copy-start.1
  147.7 2.1 %copy.13 = f32[1,16,64,1024]{3,2,1,0:T(8,128)} copy(f32[1,16,64,1024]{3,2,1,0:T(8,128)S(1)} %bitcast.8) | data formatting | bytes 8388608
  149.8 1.0 copy-done.1
  150.8 1.3 copy.14
Async XLA Ops:
  142.7 5.0 %copy-start = (f32[16,64,1024]{2,1,0:T(8,128)S(1)}, f32[16,64,1024]{2,1,0:T(8,128)}, u32[]{:S(2)}) copy-start(f32[16,64,1024]{2,1,0:T(8,128)} %get-tuple-element.7) | copy-start | bytes 12582916
  147.7 3.1 %copy-start.1 = (bf16[512,2048]{1,0:T(8,128)(2,1)S(1)}, bf16[512,2048]{1,0:T(8,128)(2,1)}, u32[]{:S(2)}) copy-start(bf16[512,2048]{1,0:T(8,128)(2,1)} %get-tuple-element.8) | copy-start | bytes 6291460

commit v2 on v0

v2 whole, which is shorter than its diff:
```python
import jax
import jax.numpy as jnp
from jax import lax
from jax.experimental import pallas as pl
from jax.experimental.pallas import tpu as pltpu
from jax.sharding import PartitionSpec as P

MESH = pl.DeviceIdType.MESH
ORDER = [
    (2, 2, 1), (0, 1, 0), (3, 2, 1), (0, 3, 0), (1, 2, 1), (1, 0, 0), (2, 3, 1), (3, 0, 0),
    (2, 1, 1), (0, 0, 1), (2, 2, 0), (1, 1, 0), (2, 1, 0), (3, 3, 0), (2, 3, 0), (1, 3, 0),
    (1, 2, 0), (0, 3, 1), (3, 2, 0), (3, 1, 0), (1, 1, 1), (0, 1, 1), (3, 3, 1), (2, 0, 0),
    (3, 1, 1), (3, 0, 1), (1, 3, 1), (0, 2, 0), (2, 0, 1), (1, 0, 1), (0, 2, 1),
]
PIECES = 4
GROUP = 16


def shifted(me, step):
    y, z, x = step
    return (
        lax.rem(me // 8 + y, 4) * 8
        + lax.rem(lax.rem(me // 2, 4) + z, 4) * 2
        + lax.rem(lax.rem(me, 2) + x, 2)
    )


def kernel(
    delta, params, moment, table_t, ids, chosen,
    par, mom, acts,
    pieces, fresh, sending, weight,
    columns, table, id_own, id_all, id_scalar, gathered, leaving, lower, upper,
    x_first, total, squares,
    local_sem, id_sem, delta_send, delta_recv, weight_send, weight_recv,
    lower_send, lower_recv, upper_send, upper_recv, forward_send, forward_recv,
    core_sem, level_send, level_recv,
):
    me = lax.axis_index("path")
    sec = lax.axis_index("section")
    half = lax.rem(sec, 2)
    mate = sec + 1 - 2 * half
    paths, rows, wide = pieces.shape
    modules = par.shape[0]
    width = table.shape[1]
    model = acts.shape[1]
    mid = model // 2
    cut_of = wide // PIECES
    others = paths - 1
    late = sec >= 2
    looks = half == 1
    holds_upper = me >= paths // 2
    reads = jnp.logical_or(late, holds_upper)
    twin = me + 1 - 2 * lax.rem(me, 2)

    def remote(src, dst, send, recv, path, section):
        return pltpu.make_async_remote_copy(
            src_ref=src, dst_ref=dst, send_sem=send, recv_sem=recv,
            device_id=(path, section), device_id_type=MESH,
        )

    def same(ref, send, recv):
        return remote(ref, ref, send, recv, me, sec)

    loads = [
        pltpu.make_async_copy(table_t, columns, local_sem.at[0]),
        pltpu.make_async_copy(params, par, local_sem.at[1]),
        pltpu.make_async_copy(moment, mom, local_sem.at[2]),
    ]
    for load in loads:
        load.start()
    cuts = [pl.ds(piece * cut_of, cut_of) for piece in range(PIECES)]
    own = [
        pltpu.make_async_copy(delta.at[me, :, cuts[piece]], pieces.at[me, :, cuts[piece]], local_sem.at[3 + piece])
        for piece in range(PIECES)
    ]
    for copy in own:
        copy.start()
    tiles = ids.shape[1] // 128
    for tile in range(tiles):
        id_own[tile:tile + 1, :] = ids[:, 128 * tile:128 * (tile + 1)]
    id_own[tiles:, :] = jnp.zeros((8 - tiles, 128), jnp.int32)
    id_all[me] = id_own[...]

    barrier = pltpu.get_barrier_semaphore()
    for step in ORDER:
        pl.semaphore_signal(barrier, inc=1, device_id=(shifted(me, step), sec), device_id_type=MESH)

    @pl.when(sec > 0)
    def _():
        pl.semaphore_signal(barrier, inc=1, device_id=(me, sec - 1), device_id_type=MESH)

    @pl.when(sec < 3)
    def _():
        pl.semaphore_signal(barrier, inc=1, device_id=(me, sec + 1), device_id_type=MESH)

    @pl.when(jnp.logical_or(sec == 0, sec == 3))
    def _():
        pl.semaphore_signal(barrier, inc=1, device_id=(twin, 3 - sec), device_id_type=MESH)

    pl.semaphore_wait(barrier, others + 2)

    @pl.when(looks)
    def _():
        for step in ORDER:
            remote(id_own, id_all.at[me], id_sem.at[0], id_sem.at[1], shifted(me, step), sec).start()

    def send_delta(piece):
        for step in ORDER:
            to = shifted(me, step)
            remote(
                delta.at[to, :, cuts[piece]], pieces.at[me, :, cuts[piece]],
                delta_send.at[piece], delta_recv.at[piece], to, sec,
            ).start()

    ahead = PIECES // 2
    for piece in range(ahead):
        send_delta(piece)

    tokens = gathered.shape[0]
    half_paths = paths // 2
    slot = lax.rem(me, half_paths)
    own_rows = pl.ds(pl.multiple_of(slot * width, width), width)
    everyone = id_all.at[pl.ds(0, others)]
    quarters = 4
    holders = half_paths // quarters
    spans = [pl.ds(at * holders * width, holders * width) for at in range(quarters)]

    @pl.when(looks)
    def _():
        loads[0].wait()

        @pl.loop(0, table.shape[0] // 640)
        def _(block):
            start = pl.multiple_of(block * 640, 640)
            table[pl.ds(start, 640), :] = columns[:, pl.ds(start, 640)].T.astype(jnp.float32)

        same(everyone, id_sem.at[0], id_sem.at[1]).wait_recv()
        ids_in = pltpu.make_async_copy(id_all, id_scalar, local_sem.at[0])
        ids_in.start()
        ids_in.wait()

        @pl.when(reads)
        def _():
            @pl.loop(0, paths)
            def _(turn):
                to = shifted(me, (turn // 8, lax.rem(turn // 2, 4), lax.rem(turn, 2)))
                to_twin = to + 1 - 2 * lax.rem(to, 2)

                @pl.loop(0, tokens // 16)
                def _(group):
                    line = group // 8
                    first = lax.rem(group, 8) * 16
                    for at in range(16):
                        token = id_scalar[to, line, first + at]
                        gathered[pl.ds(group * 16 + at, 1), :] = table[pl.ds(token, 1), :]

                leaving[to] = gathered[...].T.astype(jnp.bfloat16)

                @pl.when(jnp.logical_and(to_twin != me, jnp.logical_not(holds_upper)))
                def _():
                    remote(
                        leaving.at[to], lower.at[own_rows],
                        lower_send, lower_recv.at[slot // holders], to_twin, sec,
                    ).start()

                @pl.when(jnp.logical_and(to != me, holds_upper))
                def _():
                    remote(leaving.at[to], upper.at[own_rows], upper_send, upper_recv, to, sec).start()

        @pl.when(holds_upper)
        def _():
            upper[own_rows, :] = leaving[me]

        @pl.when(jnp.logical_and(sec == 3, jnp.logical_not(holds_upper)))
        def _():
            lower[own_rows, :] = leaving[twin]

    for piece in range(ahead, PIECES):
        send_delta(piece)

    upper_copy = remote(upper, upper, core_sem.at[0], core_sem.at[1], me, mate)

    def passing(at):
        return remote(
            lower.at[spans[at]], lower.at[spans[at]], forward_send.at[at], forward_recv.at[at], twin, sec - 3
        )

    def forward():
        @pl.when(sec == 3)
        def _():
            for at in range(quarters):
                mine = jnp.logical_and(slot // holders == at, jnp.logical_not(holds_upper))

                @pl.when(mine)
                def _():
                    same(lower.at[pl.ds(0, (holders - 1) * width)], lower_send, lower_recv.at[at]).wait_recv()

                @pl.when(jnp.logical_not(mine))
                def _():
                    same(lower.at[pl.ds(0, holders * width)], lower_send, lower_recv.at[at]).wait_recv()

                passing(at).start()

        @pl.when(holds_upper)
        def _():
            same(upper.at[pl.ds(0, mid - width)], upper_send, upper_recv).wait_recv()

        @pl.when(jnp.logical_not(holds_upper))
        def _():
            same(upper, upper_send, upper_recv).wait_recv()

        upper_copy.start()

    loads[1].wait()
    loads[2].wait()
    pair_rows, pair_cols = modules * GROUP, paths * GROUP
    col = lax.broadcasted_iota(jnp.int32, (1, pair_cols), 1)
    uses = jnp.zeros((1, pair_cols), jnp.int32)
    for path in range(paths):
        uses = jnp.where(col // GROUP == path, chosen[path], uses)
    row = lax.broadcasted_iota(jnp.int32, (pair_rows, pair_cols), 0)
    cols = lax.broadcasted_iota(jnp.int32, (pair_rows, pair_cols), 1)
    match = (uses == row // GROUP) & (lax.rem(row, GROUP) == lax.rem(cols, GROUP))
    match = match.astype(jnp.float32)
    counts = jnp.maximum(jnp.sum(match, axis=1, keepdims=True), 1.0)
    match = match.astype(jnp.bfloat16)
    for piece in range(PIECES):
        if piece == ahead:
            pl.when(looks)(forward)
        cut = cuts[piece]
        same(pieces.at[pl.ds(0, others), :, cut], delta_send.at[piece], delta_recv.at[piece]).wait_recv()
        own[piece].wait()

        @pl.loop(0, rows // GROUP)
        def _(group):
            at = pl.ds(pl.multiple_of(group * GROUP, GROUP), GROUP)
            terms = pieces[:, at, cut].reshape(pair_cols, cut_of)
            sums = jnp.dot(match, terms, preferred_element_type=jnp.float32)
            grad = sums / counts
            moved = 0.9 * mom[:, at, cut].reshape(pair_rows, cut_of) + grad
            stepped = par[:, at, cut].reshape(pair_rows, cut_of) - 0.7 * (grad + 0.9 * moved)
            mom[:, at, cut] = moved.reshape(modules, GROUP, cut_of)
            par[:, at, cut] = stepped.reshape(modules, GROUP, cut_of)
            fresh[:, at, :] = stepped.astype(jnp.bfloat16).reshape(modules, GROUP, cut_of)

        @pl.loop(0, paths)
        def _(path):
            sending[piece, path] = fresh[chosen[path]]

        weight[piece, me] = sending[piece, me]
        for step in ORDER:
            to = shifted(me, step)
            remote(
                sending.at[piece, to], weight.at[piece, me],
                weight_send.at[piece], weight_recv.at[piece], to, sec,
            ).start()

    def turned(src, dst):
        @pl.loop(0, mid // 256)
        def _(block):
            start = pl.multiple_of(block * 256, 256)
            dst[:, pl.ds(start, 256)] = src[pl.ds(start, 256), :].T

    @pl.when(jnp.logical_not(looks))
    def _():
        upper_copy.wait_recv()

    x_rest = acts.at[:, pl.ds(mid, mid)]
    turned(upper, x_rest)

    @pl.when(sec == 0)
    def _():
        for at in range(quarters):
            same(lower.at[spans[at]], forward_send.at[at], forward_recv.at[at]).wait_recv()
        turned(lower, x_first)

    size = x_first.shape[0]
    strip = 128

    def add_squares(ref, first):
        @pl.loop(0, size // strip)
        def _(block):
            at = pl.ds(pl.multiple_of(block * strip, strip), strip)
            held = jnp.zeros((strip, 128), jnp.float32) if first else squares[at, :]
            for start in range(0, ref.shape[1], 128):
                value = ref[at, start:start + 128].astype(jnp.float32)
                held = held + value * value
            squares[at, :] = held

    add_squares(x_rest, True)

    def weights_in(piece):
        same(weight.at[piece, pl.ds(0, others)], weight_send.at[piece], weight_recv.at[piece]).wait_recv()

    per = half_paths // PIECES

    def rest_part(piece):
        total[:, cuts[piece]] = jnp.dot(
            acts[:, mid:], weight[piece, half_paths:].reshape(mid, cut_of),
            preferred_element_type=jnp.float32,
        )

    def first_part(piece, sources):
        lo, hi = sources[0], sources[-1] + 1
        total[:, cuts[piece]] += jnp.dot(
            x_first[:, lo * cut_of:hi * cut_of],
            weight[piece, lo * per:hi * per].reshape((hi - lo) * cut_of, cut_of),
            preferred_element_type=jnp.float32,
        )

    def set_scale():
        @pl.loop(0, size // strip)
        def _(block):
            at = pl.ds(pl.multiple_of(block * strip, strip), strip)
            mean = jnp.sum(squares[at, :], axis=-1, keepdims=True) / model
            squares[at, :] = jnp.broadcast_to(lax.rsqrt(mean + 1e-06), (strip, 128))

    def write(piece):
        @pl.loop(0, size // strip)
        def _(block):
            at = pl.ds(pl.multiple_of(block * strip, strip), strip)
            scale = squares[at, :]
            for start in range(piece * cut_of, (piece + 1) * cut_of, 128):
                cut = pl.ds(start, 128)
                mixed = total[at, cut] * scale
                written = x_first[at, cut].astype(jnp.float32) + jax.nn.silu(mixed)
                acts[at, cut] = written.astype(jnp.bfloat16)

    def hop(piece):
        return remote(
            acts.at[:, cuts[piece]], x_first.at[:, cuts[piece]],
            level_send.at[piece], level_recv.at[piece], me, jnp.minimum(sec + 1, 3),
        )

    everything = list(range(PIECES))

    @pl.when(sec == 0)
    def _():
        add_squares(x_first, False)
        set_scale()
        for piece in everything:
            weights_in(piece)
            rest_part(piece)
            first_part(piece, everything)
            write(piece)
            hop(piece).start()

    @pl.when(sec == 1)
    def _():
        soon = PIECES // 2
        for piece in everything[:soon]:
            weights_in(piece)
            rest_part(piece)
        for source in everything:
            hop(source).wait_recv()
            add_squares(x_first.at[:, cuts[source]], False)
        set_scale()
        for piece in everything:
            if piece >= soon:
                weights_in(piece)
                rest_part(piece)
            first_part(piece, everything)
            write(piece)
            hop(piece).start()

    @pl.when(late)
    def _():
        for piece in everything:
            weights_in(piece)
            rest_part(piece)
        for source in everything[:-1]:
            hop(source).wait_recv()
            add_squares(x_first.at[:, cuts[source]], False)
        for piece in everything:
            first_part(piece, everything[:-1])
        hop(everything[-1]).wait_recv()
        add_squares(x_first.at[:, cuts[-1]], False)
        set_scale()
        for piece in everything:
            first_part(piece, everything[-1:])
            write(piece)

            @pl.when(sec == 2)
            def _():
                hop(piece).start()

    for piece in everything:
        same(pieces.at[pl.ds(0, others), :, cuts[piece]], delta_send.at[piece], delta_recv.at[piece]).wait_send()
        same(weight.at[piece, pl.ds(0, others)], weight_send.at[piece], weight_recv.at[piece]).wait_send()

        @pl.when(sec < 3)
        def _():
            hop(piece).wait_send()

    @pl.when(jnp.logical_not(looks))
    def _():
        loads[0].wait()

    @pl.when(looks)
    def _():
        same(everyone, id_sem.at[0], id_sem.at[1]).wait_send()
        upper_copy.wait_send()
        sent = leaving.at[pl.ds(0, others)]

        @pl.when(holds_upper)
        def _():
            same(sent, upper_send, upper_recv).wait_send()

        @pl.when(sec == 3)
        def _():
            for at in range(quarters):
                passing(at).wait_send()

            @pl.when(jnp.logical_not(holds_upper))
            def _():
                same(sent, lower_send, lower_recv.at[0]).wait_send()


def store(a, b, c, x, y, z, sem):
    copies = [
        pltpu.make_async_copy(src, dst, sem.at[at])
        for at, (src, dst) in enumerate(((a, x), (b, y), (c, z)))
    ]
    for copy in copies:
        copy.start()
    for copy in copies:
        copy.wait()


def local(delta, outer_params, momentum, module_table, token_ids, embedding):
    paths = module_table.shape[1]
    _, modules, rows, wide = outer_params.shape
    vocab, width = embedding.shape
    tok = token_ids.shape[1]
    model = delta.shape[2]
    mid = model // 2
    cut_of = wide // PIECES
    bf16, f32 = jnp.bfloat16, jnp.float32
    anywhere = pl.BlockSpec(memory_space=pl.ANY)
    near = pl.BlockSpec(memory_space=pltpu.VMEM)
    dma = pltpu.SemaphoreType.DMA
    held = pl.pallas_call(
        kernel,
        out_shape=(
            pltpu.VMEM((modules, rows, wide), f32),
            pltpu.VMEM((modules, rows, wide), f32),
            pltpu.VMEM((tok, model), bf16),
        ),
        in_specs=[anywhere, anywhere, anywhere, anywhere, near, pl.BlockSpec(memory_space=pltpu.SMEM)],
        out_specs=(near, near, near),
        scratch_shapes=[
            pltpu.VMEM((paths, rows, wide), bf16),
            pltpu.VMEM((modules, rows, cut_of), bf16),
            pltpu.VMEM((PIECES, paths, rows, cut_of), bf16),
            pltpu.VMEM((PIECES, paths, rows, cut_of), bf16),
            pltpu.VMEM((width, vocab), bf16),
            pltpu.VMEM((vocab, width), f32),
            pltpu.VMEM((8, 128), jnp.int32),
            pltpu.VMEM((paths, 8, 128), jnp.int32),
            pltpu.SMEM((paths, 8, 128), jnp.int32),
            pltpu.VMEM((tok, width), f32),
            pltpu.VMEM((paths, width, tok), bf16),
            pltpu.VMEM((mid, tok), bf16),
            pltpu.VMEM((mid, tok), bf16),
            pltpu.VMEM((tok, mid), bf16),
            pltpu.VMEM((tok, wide), f32),
            pltpu.VMEM((tok, 128), f32),
            dma((8,)), dma((2,)), dma((PIECES,)), dma((PIECES,)), dma((PIECES,)), dma((PIECES,)),
            dma, dma((4,)), dma, dma, dma((4,)), dma((4,)),
            dma((2,)), dma((PIECES,)), dma((PIECES,)),
        ],
        compiler_params=pltpu.CompilerParams(
            collective_id=0, has_side_effects=True, vmem_limit_bytes=46 * 1024 * 1024,
        ),
        name="outer_step",
    )(
        delta.reshape(paths, rows, wide), outer_params[0], momentum[0],
        embedding.T, token_ids, module_table[0, :, 0],
    )
    held = [pltpu.with_memory_space_constraint(value, pltpu.VMEM) for value in held]
    new_params, new_moment, acts = pl.pallas_call(
        store,
        out_shape=tuple(jax.ShapeDtypeStruct(value.shape, value.dtype) for value in held),
        in_specs=[near, near, near],
        out_specs=(anywhere, anywhere, anywhere),
        scratch_shapes=[dma((3,))],
        compiler_params=pltpu.CompilerParams(vmem_limit_bytes=2 * 1024 * 1024),
        name="store",
    )(*held)
    return (new_params[None], new_moment[None], acts[None, None])


def solution(mesh):
    return jax.shard_map(
        local,
        mesh=mesh,
        in_specs=(
            P("section", "path", None, None),
            P("section", None, "path", None),
            P("section", None, "path", None),
            P("section", None, None),
            P("path", None),
            P(None, "path"),
        ),
        out_specs=(
            P("section", None, "path", None),
            P("section", None, "path", None),
            P("section", "path", None, None),
        ),
        check_vma=False,
    )
```

time: 484 us -> 134 us (0.28)
  the two profiles are of different devices: /device:TPU:1 before, /device:TPU:21 now
where the time goes in v2:
time: 134 us
  Pallas kernels  133 us (99%)
    pallas_call x1, Pallas kernels, local(): pl.pallas_call(kernel, out_shape=(pltpu.VMEM((modules, rows, wide), f32),...  129 us
    pallas_call x1, Pallas kernels, local(): pl.pallas_call(store, out_shape=tuple((jax.ShapeDtypeStruct(value.shape,...  3.99 us

profile of v2, /device:TPU:21, one launch (start us, length us, event | category | flops | bytes accessed | tf_op | source)
XLA Modules:
  0.0 133.8 jit_solution(16103973417527151048)
XLA Ops:
  0.6 129.1 %outer_step.1 = (f32[16,64,1024]{2,1,0:T(8,128)S(1)}, f32[16,64,1024]{2,1,0:T(8,128)S(1)}, bf16[512,2048]{1,0:T(8,128)(2,1)S(1)}) custom-call(bf16[32,64,1024]{2,1,0:T(8,128)(2,1)} %bitcast.8, f32[16,64,1024]{2,1,0:T(8,128)} %bitcast.9, f32[16,64,1024]{2,1,0:T(8,128)} %bitcast.10, bf16[64,16000]{1,0:T(8,128)(2,1)} %bitcast.11, s32[1,512]{1,0:T(1,128)} %ids.1, ...), custom_call_target="tpu_custom_call" | custom-call | tf_op jit(solution)/shard_map/outer_step/pallas_call | solution.py:442
  129.8 4.0 %store.1 = (f32[16,64,1024]{2,1,0:T(8,128)}, f32[16,64,1024]{2,1,0:T(8,128)}, bf16[512,2048]{1,0:T(8,128)(2,1)}) custom-call(f32[16,64,1024]{2,1,0:T(8,128)S(1)} %get-tuple-element.9.a, f32[16,64,1024]{2,1,0:T(8,128)S(1)} %get-tuple-element.10.b, bf16[512,2048]{1,0:T(8,128)(2,1)S(1)} %get-tuple-element.11.c), custom_call_target="tpu_custom_call" | custom-call | tf_op jit(solution)/shard_map/store/pallas_call | solution.py:481

commit v3 on v2

--- a/solution.py
+++ b/solution.py
@@ -13,6 +13,7 @@
     (3, 1, 1), (3, 0, 1), (1, 3, 1), (0, 2, 0), (2, 0, 1), (1, 0, 1), (0, 2, 1),
 ]
 PIECES = 4
+GATE = 1
 GROUP = 16
 
 
@@ -29,16 +30,14 @@
     delta, params, moment, table_t, ids, chosen,
     par, mom, acts,
     pieces, fresh, sending, weight,
-    columns, table, id_own, id_all, id_scalar, gathered, leaving, lower, upper,
+    columns, table, id_own, id_all, id_scalar, gathered, leaving, relay, lower, upper,
     x_first, total, squares,
     local_sem, id_sem, delta_send, delta_recv, weight_send, weight_recv,
-    lower_send, lower_recv, upper_send, upper_recv, forward_send, forward_recv,
-    core_sem, level_send, level_recv,
+    lookup_send, lookup_recv, cross_send, cross_recv, upper_send, upper_recv, forward_send, forward_recv,
+    level_send, level_recv, gate,
 ):
     me = lax.axis_index("path")
     sec = lax.axis_index("section")
-    half = lax.rem(sec, 2)
-    mate = sec + 1 - 2 * half
     paths, rows, wide = pieces.shape
     modules = par.shape[0]
     width = table.shape[1]
@@ -47,9 +46,8 @@
     cut_of = wide // PIECES
     others = paths - 1
     late = sec >= 2
-    looks = half == 1
-    holds_upper = me >= paths // 2
-    reads = jnp.logical_or(late, holds_upper)
+    looks = late
+    half = lax.rem(sec, 2)
     twin = me + 1 - 2 * lax.rem(me, 2)
 
     def remote(src, dst, send, recv, path, section):
@@ -93,11 +91,16 @@
     def _():
         pl.semaphore_signal(barrier, inc=1, device_id=(me, sec + 1), device_id_type=MESH)
 
-    @pl.when(jnp.logical_or(sec == 0, sec == 3))
-    def _():
-        pl.semaphore_signal(barrier, inc=1, device_id=(twin, 3 - sec), device_id_type=MESH)
-
-    pl.semaphore_wait(barrier, others + 2)
+    @pl.when(late)
+    def _():
+        pl.semaphore_signal(barrier, inc=1, device_id=(twin, 0), device_id_type=MESH)
+
+    @pl.when(sec == 0)
+    def _():
+        for target in (2, 3):
+            pl.semaphore_signal(barrier, inc=1, device_id=(twin, target), device_id_type=MESH)
+
+    pl.semaphore_wait(barrier, others + 2 + jnp.where(half == 0, 1, 0))
 
     @pl.when(looks)
     def _():
@@ -113,16 +116,20 @@
             ).start()
 
     ahead = PIECES // 2
+
+    @pl.when(sec == 1)
+    def _():
+        pl.semaphore_wait(gate, 1)
+
     for piece in range(ahead):
         send_delta(piece)
 
     tokens = gathered.shape[0]
     half_paths = paths // 2
-    slot = lax.rem(me, half_paths)
-    own_rows = pl.ds(pl.multiple_of(slot * width, width), width)
+    own_rows = pl.ds(pl.multiple_of(me * width, width), width)
     everyone = id_all.at[pl.ds(0, others)]
     quarters = 4
-    holders = half_paths // quarters
+    holders = paths // quarters
     spans = [pl.ds(at * holders * width, holders * width) for at in range(quarters)]
 
     @pl.when(looks)
@@ -139,77 +146,75 @@
         ids_in.start()
         ids_in.wait()
 
-        @pl.when(reads)
-        def _():
-            @pl.loop(0, paths)
-            def _(turn):
-                to = shifted(me, (turn // 8, lax.rem(turn // 2, 4), lax.rem(turn, 2)))
-                to_twin = to + 1 - 2 * lax.rem(to, 2)
-
-                @pl.loop(0, tokens // 16)
-                def _(group):
-                    line = group // 8
-                    first = lax.rem(group, 8) * 16
-                    for at in range(16):
-                        token = id_scalar[to, line, first + at]
-                        gathered[pl.ds(group * 16 + at, 1), :] = table[pl.ds(token, 1), :]
-
-                leaving[to] = gathered[...].T.astype(jnp.bfloat16)
-
-                @pl.when(jnp.logical_and(to_twin != me, jnp.logical_not(holds_upper)))
-                def _():
-                    remote(
-                        leaving.at[to], lower.at[own_rows],
-                        lower_send, lower_recv.at[slot // holders], to_twin, sec,
-                    ).start()
-
-                @pl.when(jnp.logical_and(to != me, holds_upper))
-                def _():
-                    remote(leaving.at[to], upper.at[own_rows], upper_send, upper_recv, to, sec).start()
-
-        @pl.when(holds_upper)
-        def _():
-            upper[own_rows, :] = leaving[me]
-
-        @pl.when(jnp.logical_and(sec == 3, jnp.logical_not(holds_upper)))
-        def _():
-            lower[own_rows, :] = leaving[twin]
+        @pl.loop(0, paths)
+        def _(turn):
+            mixed = lax.rem(turn * 13, 32)
+            to = shifted(me, (mixed // 8, lax.rem(mixed // 2, 4), lax.rem(mixed, 2)))
+            to_twin = to + 1 - 2 * lax.rem(to, 2)
+
+            @pl.loop(0, tokens // 32)
+            def _(group):
+                line = half * (tokens // 128) + group // 4
+                first = lax.rem(group, 4) * 32
+                for at in range(32):
+                    token = id_scalar[to, line, first + at]
+                    gathered[pl.ds(group * 32 + at, 1), :] = table[pl.ds(token, 1), :]
+
+            leaving[to] = gathered[...].T.astype(jnp.bfloat16)
+
+            @pl.when(to_twin != me)
+            def _():
+                remote(
+                    leaving.at[to], relay.at[own_rows],
+                    lookup_send, lookup_recv.at[me // holders], to_twin, sec,
+                ).start()
+
+        relay[own_rows, :] = leaving[twin]
+
+    def passing(at):
+        into = upper if at >= quarters // 2 else lower
+        return remote(
+            relay.at[spans[at]], into.at[half, spans[at % (quarters // 2)]],
+            forward_send.at[at], forward_recv.at[half * quarters + at], twin, 0,
+        )
+
+    def crossing(at):
+        return remote(
+            relay.at[spans[quarters // 2 + at]], upper.at[half, spans[at]],
+            cross_send.at[at], cross_recv.at[at], twin, sec,
+        )
+
+    def forward():
+        for at in (2, 3, 0, 1):
+            mine = me // holders == at
+
+            @pl.when(mine)
+            def _():
+                same(relay.at[pl.ds(0, (holders - 1) * width)], lookup_send, lookup_recv.at[at]).wait_recv()
+
+            @pl.when(jnp.logical_not(mine))
+            def _():
+                same(relay.at[pl.ds(0, holders * width)], lookup_send, lookup_recv.at[at]).wait_recv()
+
+            passing(at).start()
+            if at >= quarters // 2:
+                crossing(at - quarters // 2).start()
 
     for piece in range(ahead, PIECES):
         send_delta(piece)
-
-    upper_copy = remote(upper, upper, core_sem.at[0], core_sem.at[1], me, mate)
-
-    def passing(at):
-        return remote(
-            lower.at[spans[at]], lower.at[spans[at]], forward_send.at[at], forward_recv.at[at], twin, sec - 3
-        )
-
-    def forward():
-        @pl.when(sec == 3)
-        def _():
-            for at in range(quarters):
-                mine = jnp.logical_and(slot // holders == at, jnp.logical_not(holds_upper))
-
-                @pl.when(mine)
-                def _():
-                    same(lower.at[pl.ds(0, (holders - 1) * width)], lower_send, lower_recv.at[at]).wait_recv()
-
-                @pl.when(jnp.logical_not(mine))
-                def _():
-                    same(lower.at[pl.ds(0, holders * width)], lower_send, lower_recv.at[at]).wait_recv()
-
-                passing(at).start()
-
-        @pl.when(holds_upper)
-        def _():
-            same(upper.at[pl.ds(0, mid - width)], upper_send, upper_recv).wait_recv()
-
-        @pl.when(jnp.logical_not(holds_upper))
-        def _():
-            same(upper, upper_send, upper_recv).wait_recv()
-
-        upper_copy.start()
+        if piece == ahead:
+            pl.when(looks)(forward)
+
+    def upper_hop(at):
+        return remote(upper.at[at], upper.at[at], upper_send.at[at], upper_recv.at[at], me, 1)
+
+    mate = sec + 1 - 2 * half
+    trade = remote(upper.at[half], upper.at[half], upper_send.at[0], upper_recv.at[0], me, mate)
+
+    def exchange():
+        for at in range(2):
+            crossing(at).wait_recv()
+        trade.start()
 
     loads[1].wait()
     loads[2].wait()
@@ -225,11 +230,13 @@
     counts = jnp.maximum(jnp.sum(match, axis=1, keepdims=True), 1.0)
     match = match.astype(jnp.bfloat16)
     for piece in range(PIECES):
-        if piece == ahead:
-            pl.when(looks)(forward)
         cut = cuts[piece]
         same(pieces.at[pl.ds(0, others), :, cut], delta_send.at[piece], delta_recv.at[piece]).wait_recv()
         own[piece].wait()
+        if piece == GATE:
+            @pl.when(sec == 0)
+            def _():
+                pl.semaphore_signal(gate, inc=1, device_id=(me, sec + 1), device_id_type=MESH)
 
         @pl.loop(0, rows // GROUP)
         def _(group):
@@ -255,23 +262,39 @@
                 weight_send.at[piece], weight_recv.at[piece], to, sec,
             ).start()
 
+    pl.when(late)(exchange)
+
     def turned(src, dst):
-        @pl.loop(0, mid // 256)
-        def _(block):
-            start = pl.multiple_of(block * 256, 256)
-            dst[:, pl.ds(start, 256)] = src[pl.ds(start, 256), :].T
-
-    @pl.when(jnp.logical_not(looks))
-    def _():
-        upper_copy.wait_recv()
+        for side in range(2):
+            @pl.loop(0, mid // 256)
+            def _(block):
+                start = pl.multiple_of(block * 256, 256)
+                dst[side * tokens:(side + 1) * tokens, pl.ds(start, 256)] = src[side, pl.ds(start, 256), :].T
+
+    for at in range(2):
+        @pl.when(sec == 0)
+        def _():
+            for part in (2, 3):
+                same(upper.at[at, spans[part - 2]], forward_send.at[part], forward_recv.at[at * quarters + part]).wait_recv()
+
+            upper_hop(at).start()
+
+        @pl.when(sec == 1)
+        def _():
+            upper_hop(at).wait_recv()
+
+    @pl.when(late)
+    def _():
+        trade.wait_recv()
 
     x_rest = acts.at[:, pl.ds(mid, mid)]
     turned(upper, x_rest)
 
     @pl.when(sec == 0)
     def _():
-        for at in range(quarters):
-            same(lower.at[spans[at]], forward_send.at[at], forward_recv.at[at]).wait_recv()
+        for at in range(2):
+            for part in (0, 1):
+                same(lower.at[at, spans[part]], forward_send.at[part], forward_recv.at[at * quarters + part]).wait_recv()
         turned(lower, x_first)
 
     size = x_first.shape[0]
@@ -396,24 +419,20 @@
     def _():
         loads[0].wait()
 
+    @pl.when(sec == 0)
+    def _():
+        for at in range(2):
+            upper_hop(at).wait_send()
+
     @pl.when(looks)
     def _():
         same(everyone, id_sem.at[0], id_sem.at[1]).wait_send()
-        upper_copy.wait_send()
-        sent = leaving.at[pl.ds(0, others)]
-
-        @pl.when(holds_upper)
-        def _():
-            same(sent, upper_send, upper_recv).wait_send()
-
-        @pl.when(sec == 3)
-        def _():
-            for at in range(quarters):
-                passing(at).wait_send()
-
-            @pl.when(jnp.logical_not(holds_upper))
-            def _():
-                same(sent, lower_send, lower_recv.at[0]).wait_send()
+        same(leaving.at[pl.ds(0, others)], lookup_send, lookup_recv.at[0]).wait_send()
+        for at in range(quarters):
+            passing(at).wait_send()
+        for at in range(2):
+            crossing(at).wait_send()
+        trade.wait_send()
 
 
 def store(a, b, c, x, y, z, sem):
@@ -458,16 +477,17 @@
             pltpu.VMEM((8, 128), jnp.int32),
             pltpu.VMEM((paths, 8, 128), jnp.int32),
             pltpu.SMEM((paths, 8, 128), jnp.int32),
-            pltpu.VMEM((tok, width), f32),
-            pltpu.VMEM((paths, width, tok), bf16),
-            pltpu.VMEM((mid, tok), bf16),
-            pltpu.VMEM((mid, tok), bf16),
+            pltpu.VMEM((tok // 2, width), f32),
+            pltpu.VMEM((paths, width, tok // 2), bf16),
+            pltpu.VMEM((model, tok // 2), bf16),
+            pltpu.VMEM((2, mid, tok // 2), bf16),
+            pltpu.VMEM((2, mid, tok // 2), bf16),
             pltpu.VMEM((tok, mid), bf16),
             pltpu.VMEM((tok, wide), f32),
             pltpu.VMEM((tok, 128), f32),
             dma((8,)), dma((2,)), dma((PIECES,)), dma((PIECES,)), dma((PIECES,)), dma((PIECES,)),
-            dma, dma((4,)), dma, dma, dma((4,)), dma((4,)),
-            dma((2,)), dma((PIECES,)), dma((PIECES,)),
+            dma, dma((4,)), dma((2,)), dma((2,)), dma((2,)), dma((2,)), dma((4,)), dma((8,)),
+            dma((PIECES,)), dma((PIECES,)), pltpu.SemaphoreType.REGULAR,
         ],
         compiler_params=pltpu.CompilerParams(
             collective_id=0, has_side_effects=True, vmem_limit_bytes=46 * 1024 * 1024,

time: 134 us -> 138 us (1.030); the launches traced: 134 us -> 136 us
  Pallas kernels: 133 us -> 136 us
    pallas_call x1, Pallas kernels: 129 us -> 132 us  [local(): pl.pallas_call(kernel, out_shape=(pltpu.VMEM((modules, rows, wide), f32),...]
where the time goes in v3:
time: 138 us; the launch traced here: 136 us
  Pallas kernels  136 us (99%)
    pallas_call x1, Pallas kernels, local(): pl.pallas_call(kernel, out_shape=(pltpu.VMEM((modules, rows, wide), f32),...  132 us
    pallas_call x1, Pallas kernels, local(): pl.pallas_call(store, out_shape=tuple((jax.ShapeDtypeStruct(value.shape,...  3.99 us

profile of v3, /device:TPU:21, one launch (start us, length us, event | category | flops | bytes accessed | tf_op | source)
XLA Modules:
  0.0 136.3 jit_solution(11200151594722833660)
XLA Ops:
  0.6 131.7 %outer_step.1 = (f32[16,64,1024]{2,1,0:T(8,128)S(1)}, f32[16,64,1024]{2,1,0:T(8,128)S(1)}, bf16[512,2048]{1,0:T(8,128)(2,1)S(1)}) custom-call(bf16[32,64,1024]{2,1,0:T(8,128)(2,1)} %bitcast.8, f32[16,64,1024]{2,1,0:T(8,128)} %bitcast.9, f32[16,64,1024]{2,1,0:T(8,128)} %bitcast.10, bf16[64,16000]{1,0:T(8,128)(2,1)} %bitcast.11, s32[1,512]{1,0:T(1,128)} %ids.1, ...), custom_call_target="tpu_custom_call" | custom-call | tf_op jit(solution)/shard_map/outer_step/pallas_call | solution.py:461
  132.3 4.0 %store.1 = (f32[16,64,1024]{2,1,0:T(8,128)}, f32[16,64,1024]{2,1,0:T(8,128)}, bf16[512,2048]{1,0:T(8,128)(2,1)}) custom-call(f32[16,64,1024]{2,1,0:T(8,128)S(1)} %get-tuple-element.9.a, f32[16,64,1024]{2,1,0:T(8,128)S(1)} %get-tuple-element.10.b, bf16[512,2048]{1,0:T(8,128)(2,1)S(1)} %get-tuple-element.11.c), custom_call_target="tpu_custom_call" | custom-call | tf_op jit(solution)/shard_map/store/pallas_call | solution.py:501

commit v4 on v2

--- a/solution.py
+++ b/solution.py
@@ -112,7 +112,7 @@
                 delta_send.at[piece], delta_recv.at[piece], to, sec,
             ).start()
 
-    ahead = PIECES // 2
+    ahead = PIECES - 1
     for piece in range(ahead):
         send_delta(piece)
 
@@ -143,16 +143,17 @@
         def _():
             @pl.loop(0, paths)
             def _(turn):
-                to = shifted(me, (turn // 8, lax.rem(turn // 2, 4), lax.rem(turn, 2)))
+                mixed = lax.rem(turn * 13, 32)
+                to = shifted(me, (mixed // 8, lax.rem(mixed // 2, 4), lax.rem(mixed, 2)))
                 to_twin = to + 1 - 2 * lax.rem(to, 2)
 
-                @pl.loop(0, tokens // 16)
+                @pl.loop(0, tokens // 64)
                 def _(group):
-                    line = group // 8
-                    first = lax.rem(group, 8) * 16
-                    for at in range(16):
+                    line = group // 2
+                    first = lax.rem(group, 2) * 64
+                    for at in range(64):
                         token = id_scalar[to, line, first + at]
-                        gathered[pl.ds(group * 16 + at, 1), :] = table[pl.ds(token, 1), :]
+                        gathered[pl.ds(group * 64 + at, 1), :] = table[pl.ds(token, 1), :]
 
                 leaving[to] = gathered[...].T.astype(jnp.bfloat16)
 
@@ -225,7 +226,7 @@
     counts = jnp.maximum(jnp.sum(match, axis=1, keepdims=True), 1.0)
     match = match.astype(jnp.bfloat16)
     for piece in range(PIECES):
-        if piece == ahead:
+        if piece == PIECES // 2:
             pl.when(looks)(forward)
         cut = cuts[piece]
         same(pieces.at[pl.ds(0, others), :, cut], delta_send.at[piece], delta_recv.at[piece]).wait_recv()

time: 134 us -> 133 us (level)
  no operation moved by 1% of the time
where the time goes in v4:
time: 133 us
  Pallas kernels  132 us (99%)
    pallas_call x1, Pallas kernels, local(): pl.pallas_call(kernel, out_shape=(pltpu.VMEM((modules, rows, wide), f32),...  128 us
    pallas_call x1, Pallas kernels, local(): pl.pallas_call(store, out_shape=tuple((jax.ShapeDtypeStruct(value.shape,...  3.99 us

profile of v4, /device:TPU:21, one launch (start us, length us, event | category | flops | bytes accessed | tf_op | source)
XLA Modules:
  0.0 133.0 jit_solution(7883223543687720718)
XLA Ops:
  0.6 128.4 %outer_step.1 = (f32[16,64,1024]{2,1,0:T(8,128)S(1)}, f32[16,64,1024]{2,1,0:T(8,128)S(1)}, bf16[512,2048]{1,0:T(8,128)(2,1)S(1)}) custom-call(bf16[32,64,1024]{2,1,0:T(8,128)(2,1)} %bitcast.8, f32[16,64,1024]{2,1,0:T(8,128)} %bitcast.9, f32[16,64,1024]{2,1,0:T(8,128)} %bitcast.10, bf16[64,16000]{1,0:T(8,128)(2,1)} %bitcast.11, s32[1,512]{1,0:T(1,128)} %ids.1, ...), custom_call_target="tpu_custom_call" | custom-call | tf_op jit(solution)/shard_map/outer_step/pallas_call | solution.py:443
  129.1 4.0 %store.1 = (f32[16,64,1024]{2,1,0:T(8,128)}, f32[16,64,1024]{2,1,0:T(8,128)}, bf16[512,2048]{1,0:T(8,128)(2,1)}) custom-call(f32[16,64,1024]{2,1,0:T(8,128)S(1)} %get-tuple-element.9.a, f32[16,64,1024]{2,1,0:T(8,128)S(1)} %get-tuple-element.10.b, bf16[512,2048]{1,0:T(8,128)(2,1)S(1)} %get-tuple-element.11.c), custom_call_target="tpu_custom_call" | custom-call | tf_op jit(solution)/shard_map/store/pallas_call | solution.py:482
